TPU v7x, 256 devices: a whole 4x4x8 slice. The times are simulated.
256 devices in a mesh: row: 64 (over y, z, core), col: 4 (over x).
Axes of the slice: x: 4, y: 4, z: 8, core: 2. Of those that a mesh axis runs over, the one named last changes fastest.
Arguments:
- right_side: float32 [3, 65536, 512], P(None, 'row', 'col'), may hold values from -48 to 48
- onsite: float32 [65536], P('row'), may hold values from 8 to 16
- energies: float32 [512], P('col'), may hold values from -1 to -0.25
- ks_tiles: bfloat16 [512, 24, 128, 128], P('row'), may hold values from -1 to 1
- correlation_tiles: bfloat16 [512, 8, 128, 128], P('row'), may hold values from -0.1875 to 0.1875
- tile_slot: int32 [512, 24], P('row'), may hold values from 0 to 27, as said below
- readers: int32 [64, 7, 4], P('row'), may hold values from 0 to 7, as said below
Outputs:
- solution_field: float32 [3, 65536, 512], P(None, 'row', 'col')
- residual: float32 [3, 65536, 512], P(None, 'row', 'col')
Inputs may be any that keep to these rules, and one draw needn't show every extreme that they name: readers[p, o] holds 4 distinct local cluster numbers of row device p; they are read by the row device whose index is p - o + 3, cyclically. `tile_slot`: slots are distinct within one cluster row; on each row device every slot is named by some tile.
All inputs are finite; a program needn't handle non-finite values.
Results may differ from a plain program's by a relative error of at most 0.0023.
Values may be sent and summed in bfloat16 or wider, within the bound.
A program may use at most 128 MiB of HBM per device.

v0:
```python
import jax
import jax.numpy as jnp
from jax import lax
from jax.sharding import PartitionSpec as P

ITERS = 2


def shifted(array, axis, by):
    count = lax.axis_size(axis)
    return lax.ppermute(array, axis, [(i, (i + by) % count) for i in range(count)])


def body(right_side, onsite, energies, ks_tiles, correlation_tiles, tile_slot, readers):
    fields, rows, orbitals = right_side.shape
    clusters, tiles_row, width, _ = ks_tiles.shape
    tiles_correlation = correlation_tiles.shape[1]
    span = readers.shape[1]
    served = readers.shape[2]
    middle = (span - 1) // 2
    slots = span * served
    onehot = (tile_slot[:, :, None] == jnp.arange(slots, dtype=jnp.int32)[None, None, :]).astype(
        jnp.bfloat16
    )
    dense_ks = jnp.einsum("cks,ckab->casb", onehot, ks_tiles, preferred_element_type=jnp.float32)
    dense_ks = dense_ks.astype(jnp.bfloat16).reshape(clusters * width, slots * width)
    correlation_slot = tile_slot[:, :tiles_correlation]

    def squares(vector):
        return lax.psum(jnp.sum(vector * vector, axis=(1, 2)), ("row", "col"))

    solution_field = jnp.zeros_like(right_side)
    residual = right_side
    direction = right_side
    norm_now = squares(residual)
    for step in range(ITERS):
        blocks = direction.astype(jnp.bfloat16).reshape(fields, clusters, width, orbitals)
        outgoing = blocks[:, readers[0]]
        pieces = []
        for offset in range(span):
            if offset == middle:
                pieces.append(outgoing[:, offset])
            else:
                pieces.append(shifted(outgoing[:, offset], "row", middle - offset))
        received = jnp.stack(pieces, 1)
        gathered = received.reshape(fields, slots * width, orbitals)
        ks_part = jnp.einsum("rk,fkj->frj", dense_ks, gathered, preferred_element_type=jnp.float32)
        picked = gathered.reshape(fields, slots, width, orbitals)[:, correlation_slot]
        ov_part = jnp.einsum(
            "ckab,fckbj->fcaj", correlation_tiles, picked, preferred_element_type=jnp.float32
        )
        ov_part = ov_part.reshape(fields, rows, orbitals)
        image = onsite[None, :, None] * direction + (ks_part - ov_part * energies[None, None, :])
        bend = lax.psum(jnp.sum(direction * image, axis=(1, 2)), ("row", "col"))
        alpha = (norm_now / bend)[:, None, None]
        solution_field = solution_field + alpha * direction
        residual = residual - alpha * image
        norm_next = squares(residual)
        direction = residual + (norm_next / norm_now)[:, None, None] * direction
        norm_now = norm_next
    return (solution_field, residual)


def solution(mesh):
    placed = (
        P(None, "row", "col"),
        P("row"),
        P("col"),
        P("row", None, None, None),
        P("row", None, None, None),
        P("row", None),
        P("row", None, None),
    )
    return jax.shard_map(
        body,
        mesh=mesh,
        in_specs=placed,
        out_specs=(P(None, "row", "col"), P(None, "row", "col")),
        check_vma=False,
    )
```

profile of v0, /device:TPU:1, one launch (start us, length us, event | category | flops | bytes accessed | tf_op | source)
XLA Modules:
  0.0 480.4 jit_solution(6264991138397080473)
XLA Ops:
  15.0 16.7 %collective-permute-done = bf16[3,4,128,128]{3,2,0,1:T(8,128)(2,1)S(1)} collective-permute-done((bf16[3,4,128,128]{3,2,0,1:T(8,128)(2,1)S(1)}, bf16[3,4,128,128]{3,2,0,1:T(8,128)(2,1)S(1)}, u32[]{:S(2)}, u32[]{:S(2)}) %collective-permute-start) | collective-permute-done | bytes 393248 | tf_op jit(solution)/shard_map/ppermute | solution.py:11
  32.4 6.9 %collective-permute-done.1 = bf16[3,4,128,128]{3,2,0,1:T(8,128)(2,1)S(1)} collective-permute-done((bf16[3,4,128,128]{3,2,0,1:T(8,128)(2,1)S(1)}, bf16[3,4,128,128]{3,2,0,1:T(8,128)(2,1)S(1)}, u32[]{:S(2)}, u32[]{:S(2)}) %collective-permute-start.1) | collective-permute-done | bytes 393248 | tf_op jit(solution)/shard_map/ppermute | solution.py:11
  47.2 11.1 %convert_bitcast_fusion = bf16[8,128,28,128]{3,2,1,0:T(8,128)(2,1)} fusion(bf16[8,24,128,128]{3,2,1,0:T(8,128)(2,1)} %param.10, s32[8,24]{1,0:T(8,128)S(1)} %copy-done.4), kind=kOutput, calls=%fused_computation.4 | convolution fusion | flops 179836160 | bytes 13632256 | tf_op jit(solution)/shard_map/cks,ckab->casb/dot_general | solution.py:25
  61.4 12.8 %reshape.105 = bf16[1024,3584,1]{1,0,2:T(8,128)(2,1)} reshape(bf16[8,128,28,128]{3,2,1,0:T(8,128)(2,1)} %convert_bitcast_fusion) | data formatting | bytes 14680064 | tf_op jit(solution)/shard_map/reshape | solution.py:26
  79.7 9.9 %collective-permute-done.5 = bf16[3,4,128,128]{3,2,0,1:T(8,128)(2,1)S(1)} collective-permute-done((bf16[3,4,128,128]{3,2,0,1:T(8,128)(2,1)S(1)}, bf16[3,4,128,128]{3,2,0,1:T(8,128)(2,1)S(1)}, u32[]{:S(2)}, u32[]{:S(2)}) %collective-permute-start.5) | collective-permute-done | bytes 393248 | tf_op jit(solution)/shard_map/ppermute | solution.py:11
  94.0 6.1 %copy.35 = bf16[3,7,4,128,128]{3,2,1,4,0:T(4,128)(2,1)} copy(bf16[3,7,4,128,128]{4,3,0,2,1:T(8,128)(2,1)} %bitcast_dynamic-update-slice_fusion.6) | data formatting | bytes 5505024 | tf_op jit(solution)/shard_map/stack | solution.py:45
  100.2 5.6 %reshape.60 = bf16[3,3584,128]{1,2,0:T(8,128)(2,1)} reshape(bf16[3,7,4,128,128]{3,2,1,4,0:T(4,128)(2,1)} %copy.35) | data formatting | bytes 5505024 | tf_op jit(solution)/shard_map/reshape | solution.py:46
  105.7 5.7 %gather_fusion.1 = bf16[64,3,128,128]{3,2,1,0:T(8,128)(2,1)} fusion(bf16[3,28,128,128]{3,2,1,0:T(8,128)(2,1)} %bitcast.129, s32[1024]{0:T(1024)S(1)} %get-tuple-element.32), kind=kCustom, calls=%fused_computation.1 | custom fusion | bytes 12583168 | tf_op jit(solution)/shard_map/gather | solution.py:48
  111.4 5.2 %fusion.7 = f32[3,8,128,128]{3,2,0,1:T(8,128)} fusion(bf16[3,8,8,128,128]{4,3,0,2,1:T(8,128)(2,1)} %bitcast.132, bf16[8,8,128,128]{3,2,1,0:T(8,128)(2,1)S(1)} %copy-done), kind=kOutput, calls=%fused_computation.22 | convolution fusion | flops 805306368 | bytes 9961472 | tf_op jit(solution)/shard_map/ckab,fckbj->fcaj/dot_general | solution.py:49
  122.2 9.1 %multiply_reduce_fusion.2 = (f32[3]{0:T(128)S(1)}, f32[3,1024,128]{1,2,0:T(8,128)}) fusion(f32[3,1024,128]{1,2,0:T(8,128)} %copy.42, f32[3,1024,128]{1,2,0:T(8,128)} %reshape.62, f32[128]{0:T(128)S(1)} %copy-done.6, bf16[3,3584,128]{1,2,0:T(8,128)(2,1)} %reshape.60, bf16[1024,3584,1]{1,0,2:T(8,128)(2,1)} %reshape.105, f32[1024]{0:T(1024)S(1)} %copy-done.5), kind=kOutput, calls=%fused_computation.20 | convolution fusion | flops 2820931584 | bytes 14815756 | tf_op jit(solution)/shard_map/rk,fkj->frj/dot_general | solution.py:47
  131.3 76.8 %all-reduce = (f32[3]{0:T(128)S(1)}, f32[3]{0:T(128)S(1)}) all-reduce(f32[3]{0:T(128)S(1)} %get-tuple-element.26, f32[3]{0:T(128)S(1)} %get-tuple-element.28), channel_id=1, replica_groups=mesh['row'=64,'col'=4] {'row','col'}, use_global_device_ids=true, to_apply=%region_1.0 | all-reduce | flops 6 | bytes 48 | tf_op jit(solution)/shard_map/psum | solution.py:30
  210.4 73.1 %psum.30 = f32[3]{0:T(128)S(1)} all-reduce(f32[3]{0:T(128)S(1)} %multiply_reduce_fusion.1), channel_id=1, replica_groups=mesh['row'=64,'col'=4] {'row','col'}, use_global_device_ids=true, to_apply=%region_5.0 | all-reduce | flops 3 | bytes 24 | tf_op jit(solution)/shard_map/psum | solution.py:30
  294.9 15.9 %collective-permute-done.6 = bf16[3,4,128,128]{3,2,0,1:T(8,128)(2,1)S(1)} collective-permute-done((bf16[3,4,128,128]{3,2,0,1:T(8,128)(2,1)S(1)}, bf16[3,4,128,128]{3,2,0,1:T(8,128)(2,1)S(1)}, u32[]{:S(2)}, u32[]{:S(2)}) %collective-permute-start.6) | collective-permute-done | bytes 393248 | tf_op jit(solution)/shard_map/ppermute | solution.py:11
  310.8 9.6 %collective-permute-done.7 = bf16[3,4,128,128]{3,2,0,1:T(8,128)(2,1)S(1)} collective-permute-done((bf16[3,4,128,128]{3,2,0,1:T(8,128)(2,1)S(1)}, bf16[3,4,128,128]{3,2,0,1:T(8,128)(2,1)S(1)}, u32[]{:S(2)}, u32[]{:S(2)}) %collective-permute-start.7) | collective-permute-done | bytes 393248 | tf_op jit(solution)/shard_map/ppermute | solution.py:11
  320.8 4.9 %collective-permute-start.9 = (bf16[3,4,128,128]{3,2,0,1:T(8,128)(2,1)S(1)}, bf16[3,4,128,128]{3,2,0,1:T(8,128)(2,1)S(1)}, u32[]{:S(2)}, u32[]{:S(2)}) collective-permute-start(bf16[3,4,128,128]{3,2,0,1:T(8,128)(2,1)S(1)} %get-tuple-element.12), channel_id=1, source_target_pairs={{0,252},{4,0},{8,4},{12,8},{16,12},{20,16},{24,20},{28,24},{32,28}... | collective-permute-start | bytes 1179656 | tf_op jit(solution)/shard_map/ppermute | solution.py:11
  328.1 8.2 %collective-permute-done.10 = bf16[3,4,128,128]{3,2,0,1:T(8,128)(2,1)S(1)} collective-permute-done((bf16[3,4,128,128]{3,2,0,1:T(8,128)(2,1)S(1)}, bf16[3,4,128,128]{3,2,0,1:T(8,128)(2,1)S(1)}, u32[]{:S(2)}, u32[]{:S(2)}) %collective-permute-start.10) | collective-permute-done | bytes 393248 | tf_op jit(solution)/shard_map/ppermute | solution.py:11
  336.4 12.9 %collective-permute-done.11 = bf16[3,4,128,128]{3,2,0,1:T(8,128)(2,1)S(1)} collective-permute-done((bf16[3,4,128,128]{3,2,0,1:T(8,128)(2,1)S(1)}, bf16[3,4,128,128]{3,2,0,1:T(8,128)(2,1)S(1)}, u32[]{:S(2)}, u32[]{:S(2)}) %collective-permute-start.11) | collective-permute-done | bytes 393248 | tf_op jit(solution)/shard_map/ppermute | solution.py:11
  352.8 6.1 %copy.47 = bf16[3,7,4,128,128]{3,2,1,4,0:T(4,128)(2,1)} copy(bf16[3,7,4,128,128]{4,3,0,2,1:T(8,128)(2,1)} %copy-done.1) | data formatting | bytes 5505024 | tf_op jit(solution)/shard_map/stack | solution.py:45
  358.9 5.6 %reshape.64 = bf16[3,3584,128]{1,2,0:T(8,128)(2,1)} reshape(bf16[3,7,4,128,128]{3,2,1,4,0:T(4,128)(2,1)} %copy.47) | data formatting | bytes 5505024 | tf_op jit(solution)/shard_map/reshape | solution.py:46
  364.4 5.7 %gather_fusion.3 = bf16[64,3,128,128]{3,2,1,0:T(8,128)(2,1)} fusion(bf16[3,28,128,128]{3,2,1,0:T(8,128)(2,1)} %bitcast.130, s32[1024]{0:T(1024)S(1)} %get-tuple-element.32), kind=kCustom, calls=%fused_computation.3 | custom fusion | bytes 12583168 | tf_op jit(solution)/shard_map/gather | solution.py:48
  370.1 5.3 %fusion.10 = f32[3,8,128,128]{3,2,0,1:T(8,128)} fusion(bf16[3,8,8,128,128]{4,3,0,2,1:T(8,128)(2,1)} %bitcast.131, bf16[8,8,128,128]{3,2,1,0:T(8,128)(2,1)S(1)} %copy-done), kind=kOutput, calls=%fused_computation.23 | convolution fusion | flops 805306368 | bytes 9961472 | tf_op jit(solution)/shard_map/ckab,fckbj->fcaj/dot_general | solution.py:49
  381.1 9.1 %multiply_reduce_fusion = (f32[3]{0:T(128)S(1)}, f32[3,1024,128]{1,2,0:T(8,128)}) fusion(f32[3,1024,128]{1,2,0:T(8,128)} %get-tuple-element.9, f32[3,1024,128]{1,2,0:T(8,128)} %reshape.65, f32[128]{0:T(128)S(1)} %copy-done.6, bf16[3,3584,128]{1,2,0:T(8,128)(2,1)} %reshape.64, bf16[1024,3584,1]{1,0,2:T(8,128)(2,1)} %reshape.105, f32[1024]{0:T(1024)S(1)} %copy-done.5), kind=kOutput, calls=%fused_computation.16 | convolution fusion | flops 2820931584 | bytes 14815756 | tf_op jit(solution)/shard_map/rk,fkj->frj/dot_general | solution.py:47
  390.2 78.5 %psum.31 = f32[3]{0:T(128)S(1)} all-reduce(f32[3]{0:T(128)S(1)} %get-tuple-element.30), channel_id=1, replica_groups=mesh['row'=64,'col'=4] {'row','col'}, use_global_device_ids=true, to_apply=%region_7.0 | all-reduce | flops 3 | bytes 24 | tf_op jit(solution)/shard_map/psum | solution.py:54
  468.7 5.6 %multiply_subtract_fusion = (f32[3,1024,128]{1,2,0:T(8,128)}, f32[3,1024,128]{1,2,0:T(8,128)}) fusion(f32[3,1024,128]{1,2,0:T(8,128)} %get-tuple-element.31, f32[3]{0:T(128)S(1)} %div.11, f32[3,1024,128]{1,2,0:T(8,128)} %copy.42, f32[3,1024,128]{1,2,0:T(8,128)} %get-tuple-element.29, f32[3]{0:T(128)S(1)} %div.9, f32[3,1024,128]{1,2,0:T(8,128)} %get-tuple-element.9), kind=kLoop, calls=%fused_computation.14 | loop fusion | flops 2752512 | bytes 9437208 | tf_op jit(solution)/shard_map/sub | solution.py:57
  (70 shorter events, 73.2 us)
Async XLA Ops:
  0.6 110.8 %copy-start = (bf16[8,8,128,128]{3,2,1,0:T(8,128)(2,1)S(1)}, bf16[8,8,128,128]{3,2,1,0:T(8,128)(2,1)}, u32[]{:S(2)}) copy-start(bf16[8,8,128,128]{3,2,1,0:T(8,128)(2,1)} %param.11) | copy-start | bytes 6291460
  7.1 33.8 %copy-start.3 = (bf16[28,3,128,128]{3,2,1,0:T(8,128)(2,1)S(1)}, bf16[28,3,128,128]{3,2,1,0:T(8,128)(2,1)}, u32[]{:S(2)}) copy-start(bf16[28,3,128,128]{3,2,1,0:T(8,128)(2,1)} %gather_fusion) | copy-start | bytes 8257540
  8.6 23.0 %collective-permute-start = (bf16[3,4,128,128]{3,2,0,1:T(8,128)(2,1)S(1)}, bf16[3,4,128,128]{3,2,0,1:T(8,128)(2,1)S(1)}, u32[]{:S(2)}, u32[]{:S(2)}) collective-permute-start(bf16[3,4,128,128]{3,2,0,1:T(8,128)(2,1)S(1)} %get-tuple-element.23), channel_id=1, source_target_pairs={{0,12},{4,16},{8,20},{12,24},{16,28},{20,32},{24,36},{28,40},{32,4... | collective-permute-start | bytes 1179656 | tf_op jit(solution)/shard_map/ppermute | solution.py:11
  13.1 26.3 %collective-permute-start.1 = (bf16[3,4,128,128]{3,2,0,1:T(8,128)(2,1)S(1)}, bf16[3,4,128,128]{3,2,0,1:T(8,128)(2,1)S(1)}, u32[]{:S(2)}, u32[]{:S(2)}) collective-permute-start(bf16[3,4,128,128]{3,2,0,1:T(8,128)(2,1)S(1)} %get-tuple-element.22), channel_id=1, source_target_pairs={{0,8},{4,12},{8,16},{12,20},{16,24},{20,28},{24,32},{28,36},{32,40... | collective-permute-start | bytes 1179656 | tf_op jit(solution)/shard_map/ppermute | solution.py:11
  14.7 32.5 %copy-start.4 = (s32[8,24]{1,0:T(8,128)S(1)}, s32[8,24]{1,0:T(8,128)}, u32[]{:S(2)}) copy-start(s32[8,24]{1,0:T(8,128)} %param.12) | copy-start | bytes 2308
  14.7 25.4 %collective-permute-start.2 = (bf16[3,4,128,128]{3,2,0,1:T(8,128)(2,1)S(1)}, bf16[3,4,128,128]{3,2,0,1:T(8,128)(2,1)S(1)}, u32[]{:S(2)}, u32[]{:S(2)}) collective-permute-start(bf16[3,4,128,128]{3,2,0,1:T(8,128)(2,1)S(1)} %get-tuple-element.21), channel_id=1, source_target_pairs={{0,4},{4,8},{8,12},{12,16},{16,20},{20,24},{24,28},{28,32},{32,36}... | collective-permute-start | bytes 1179656 | tf_op jit(solution)/shard_map/ppermute | solution.py:11
  41.8 36.1 %collective-permute-start.4 = (bf16[3,4,128,128]{3,2,0,1:T(8,128)(2,1)S(1)}, bf16[3,4,128,128]{3,2,0,1:T(8,128)(2,1)}, u32[]{:S(2)}, u32[]{:S(2)}) collective-permute-start(bf16[3,4,128,128]{3,2,0,1:T(8,128)(2,1)S(1)} %get-tuple-element.18), channel_id=1, source_target_pairs={{0,248},{4,252},{8,0},{12,4},{16,8},{20,12},{24,16},{28,20},{32,24... | collective-permute-start | bytes 1179656 | tf_op jit(solution)/shard_map/ppermute | solution.py:11
  45.1 31.0 %collective-permute-start.3 = (bf16[3,4,128,128]{3,2,0,1:T(8,128)(2,1)S(1)}, bf16[3,4,128,128]{3,2,0,1:T(8,128)(2,1)}, u32[]{:S(2)}, u32[]{:S(2)}) collective-permute-start(bf16[3,4,128,128]{3,2,0,1:T(8,128)(2,1)S(1)} %get-tuple-element.19), channel_id=1, source_target_pairs={{0,252},{4,0},{8,4},{12,8},{16,12},{20,16},{24,20},{28,24},{32,28}... | collective-permute-start | bytes 1179656 | tf_op jit(solution)/shard_map/ppermute | solution.py:11
  74.2 15.4 %collective-permute-start.5 = (bf16[3,4,128,128]{3,2,0,1:T(8,128)(2,1)S(1)}, bf16[3,4,128,128]{3,2,0,1:T(8,128)(2,1)S(1)}, u32[]{:S(2)}, u32[]{:S(2)}) collective-permute-start(bf16[3,4,128,128]{3,2,0,1:T(8,128)(2,1)S(1)} %get-tuple-element.17), channel_id=1, source_target_pairs={{0,244},{4,248},{8,252},{12,0},{16,4},{20,8},{24,12},{28,16},{32,2... | collective-permute-start | bytes 1179656 | tf_op jit(solution)/shard_map/ppermute | solution.py:11
  116.6 5.6 %copy-start.5 = (f32[1024]{0:T(1024)S(1)}, f32[1024]{0:T(1024)}, u32[]{:S(2)}) copy-start(f32[1024]{0:T(1024)} %param.8) | copy-start | bytes 12292
  116.6 5.6 %copy-start.6 = (f32[128]{0:T(128)S(1)}, f32[128]{0:T(128)}, u32[]{:S(2)}) copy-start(f32[128]{0:T(128)} %param.9) | copy-start | bytes 1540
  291.5 29.0 %copy-start.2 = (bf16[28,3,128,128]{3,2,1,0:T(8,128)(2,1)S(1)}, bf16[28,3,128,128]{3,2,1,0:T(8,128)(2,1)}, u32[]{:S(2)}) copy-start(bf16[28,3,128,128]{3,2,1,0:T(8,128)(2,1)} %gather_fusion.2) | copy-start | bytes 8257540
  293.0 17.8 %collective-permute-start.6 = (bf16[3,4,128,128]{3,2,0,1:T(8,128)(2,1)S(1)}, bf16[3,4,128,128]{3,2,0,1:T(8,128)(2,1)S(1)}, u32[]{:S(2)}, u32[]{:S(2)}) collective-permute-start(bf16[3,4,128,128]{3,2,0,1:T(8,128)(2,1)S(1)} %get-tuple-element.16), channel_id=1, source_target_pairs={{0,12},{4,16},{8,20},{12,24},{16,28},{20,32},{24,36},{28,40},{32,4... | collective-permute-start | bytes 1179656 | tf_op jit(solution)/shard_map/ppermute | solution.py:11
  293.6 26.8 %collective-permute-start.7 = (bf16[3,4,128,128]{3,2,0,1:T(8,128)(2,1)S(1)}, bf16[3,4,128,128]{3,2,0,1:T(8,128)(2,1)S(1)}, u32[]{:S(2)}, u32[]{:S(2)}) collective-permute-start(bf16[3,4,128,128]{3,2,0,1:T(8,128)(2,1)S(1)} %get-tuple-element.15), channel_id=1, source_target_pairs={{0,8},{4,12},{8,16},{12,20},{16,24},{20,28},{24,32},{28,36},{32,40... | collective-permute-start | bytes 1179656 | tf_op jit(solution)/shard_map/ppermute | solution.py:11
  294.5 26.0 %collective-permute-start.8 = (bf16[3,4,128,128]{3,2,0,1:T(8,128)(2,1)S(1)}, bf16[3,4,128,128]{3,2,0,1:T(8,128)(2,1)S(1)}, u32[]{:S(2)}, u32[]{:S(2)}) collective-permute-start(bf16[3,4,128,128]{3,2,0,1:T(8,128)(2,1)S(1)} %get-tuple-element.14), channel_id=1, source_target_pairs={{0,4},{4,8},{8,12},{12,16},{16,20},{20,24},{24,28},{28,32},{32,36}... | collective-permute-start | bytes 1179656 | tf_op jit(solution)/shard_map/ppermute | solution.py:11
  320.8 7.3 %collective-permute-start.9 = (bf16[3,4,128,128]{3,2,0,1:T(8,128)(2,1)S(1)}, bf16[3,4,128,128]{3,2,0,1:T(8,128)(2,1)S(1)}, u32[]{:S(2)}, u32[]{:S(2)}) collective-permute-start(bf16[3,4,128,128]{3,2,0,1:T(8,128)(2,1)S(1)} %get-tuple-element.12), channel_id=1, source_target_pairs={{0,252},{4,0},{8,4},{12,8},{16,12},{20,16},{24,20},{28,24},{32,28}... | collective-permute-start | bytes 1179656 | tf_op jit(solution)/shard_map/ppermute | solution.py:11
  325.7 10.7 %collective-permute-start.10 = (bf16[3,4,128,128]{3,2,0,1:T(8,128)(2,1)S(1)}, bf16[3,4,128,128]{3,2,0,1:T(8,128)(2,1)S(1)}, u32[]{:S(2)}, u32[]{:S(2)}) collective-permute-start(bf16[3,4,128,128]{3,2,0,1:T(8,128)(2,1)S(1)} %get-tuple-element.11), channel_id=1, source_target_pairs={{0,248},{4,252},{8,0},{12,4},{16,8},{20,12},{24,16},{28,20},{32,24... | collective-permute-start | bytes 1179656 | tf_op jit(solution)/shard_map/ppermute | solution.py:11
  325.7 23.7 %collective-permute-start.11 = (bf16[3,4,128,128]{3,2,0,1:T(8,128)(2,1)S(1)}, bf16[3,4,128,128]{3,2,0,1:T(8,128)(2,1)S(1)}, u32[]{:S(2)}, u32[]{:S(2)}) collective-permute-start(bf16[3,4,128,128]{3,2,0,1:T(8,128)(2,1)S(1)} %get-tuple-element.10), channel_id=1, source_target_pairs={{0,244},{4,248},{8,252},{12,0},{16,4},{20,8},{24,12},{28,16},{32,2... | collective-permute-start | bytes 1179656 | tf_op jit(solution)/shard_map/ppermute | solution.py:11
  349.4 1.6 copy-start.1
where the time goes:
time: 482 us; the launch traced here: 480 us
  blocking collectives  228 us (47%)
  local copies, waits for them, and re-layouts  92.7 us (19%)
  waiting for transfers between devices  82.5 us (17%)
  matrix products  39.8 us (8%)
  starting transfers between devices  20.5 us (4%)
  other arithmetic  15.7 us (3%)
    psum x2, blocking collectives, squares(): return lax.psum(jnp.sum(vector * vector, axis=(1, 2)), ('row', 'col'))  150 us
    ppermute x12, waiting for transfers between devices, shifted(): lax.ppermute(array, axis, [(i, (i + by) % count) for i in range(count)])  82.5 us
    psum x1, blocking collectives, body(): bend = lax.psum(jnp.sum(direction * image, axis=(1, 2)), ('row', 'col'))  78.5 us
    ppermute x12, starting transfers between devices, shifted(): lax.ppermute(array, axis, [(i, (i + by) % count) for i in range(count)])  20.5 us
    another operation x6, local copies, waits for them, and re-layouts, body(): received = jnp.stack(pieces, 1)  18.6 us
    dot_general x2, matrix products, body(): jnp.einsum('rk,fkj->frj', dense_ks, gathered, preferred_element_type=jnp....  18.2 us
    unnamed x27, local copies, waits for them, and re-layouts  16.8 us
    reshape x1, local copies, waits for them, and re-layouts, body(): dense_ks.astype(jnp.bfloat16).reshape(clusters * width, slots * width)  12.8 us
  transfers between devices with their start and end apart: 12, of which 8 were waited for; matrix products, arithmetic and copies ran while one was open for 7% of the time, Pallas kernels for 0%

commit v1 on v0

v1 whole, which is shorter than its diff:
```python
import functools

import jax
import jax.numpy as jnp
from jax import lax
from jax.experimental import pallas as pl
from jax.experimental.pallas import tpu as pltpu
from jax.sharding import PartitionSpec as P

MESH = pl.DeviceIdType.MESH
F32 = jnp.float32
BF16 = jnp.bfloat16
ITERS = 2
SIZES = {"x": 4, "y": 4, "z": 8, "core": 2}
GROUPS = (("x", "y"), ("z", "core"))
STEP = 1.0 / 12.0
OTHERS = (0, 6, 1, 5, 2, 4)


def members(axes, here):
    count, mine = 1, 0
    for a in axes:
        count *= SIZES[a]
        mine = mine * SIZES[a] + here[a]
    found = []
    for distance in range(1, count):
        there, rest = dict(here), lax.rem(mine + distance, count)
        for a in reversed(axes):
            there[a] = lax.rem(rest, SIZES[a])
            rest = rest // SIZES[a]
        found.append(((there["y"] * SIZES["z"] + there["z"]) * SIZES["core"] + there["core"], there["x"]))
    return found


def kernel(
    right_hbm, onsite_ref, energies_ref, ks_hbm, corr_hbm, slot_ref, readers_ref,
    x_hbm, res_hbm,
    r0a, r0b, r0c, y, dd, im, ob, wb, kc, ks, corr, gath, pack, inv_v, inv_s, sums,
    part1, got1a, part1b, got1b, part2, got2a, part2b, got2b,
    load_sem, inv_sem, out_sem, send_sem, recv_sem, psend, precv,
):
    r0 = (r0a, r0b, r0c)
    fields = len(r0)
    clusters = 8
    width = 128
    slots = 28
    n_row = lax.axis_size("row")
    row, col = lax.axis_index("row"), lax.axis_index("col")
    here = {"x": col, "y": row // 16, "z": lax.rem(row // 2, 8), "core": lax.rem(row, 2)}
    groups = [members(g, here) for g in GROUPS]
    targets = {o: (lax.rem(row + 3 - o + n_row, n_row), col) for o in OTHERS}

    barrier = pltpu.get_barrier_semaphore()
    everyone = list(targets.values()) + groups[0] + groups[1]
    for device in everyone:
        pl.semaphore_signal(barrier, 1, device_id=device, device_id_type=MESH)

    loads = [pltpu.make_async_copy(right_hbm.at[f], r0[f], load_sem.at[f]) for f in range(fields)]
    loads.append(pltpu.make_async_copy(ks_hbm, ks.at[pl.ds(0, 192)], load_sem.at[3]))
    loads.append(pltpu.make_async_copy(corr_hbm, corr.at[pl.ds(0, 64)], load_sem.at[4]))
    for load in loads:
        load.start()

    lane = lax.broadcasted_iota(jnp.int32, (8, 128), 1)
    first = lax.broadcasted_iota(jnp.int32, (8, 128), 0)
    at_ks = jnp.full((8, 128), 192, jnp.int32)
    at_corr = jnp.full((8, 128), 64, jnp.int32)
    for k in range(24):
        hit = lane == slot_ref[:, k : k + 1]
        at_ks = jnp.where(hit, first * 24 + k, at_ks)
        if k < 8:
            at_corr = jnp.where(hit, first * 8 + k, at_corr)
    inv_v[0:8] = at_ks
    inv_v[8:16] = at_corr
    inv_copy = pltpu.make_async_copy(inv_v, inv_s, inv_sem)
    inv_copy.start()
    ks[192] = jnp.zeros((width, width), BF16)
    corr[64] = jnp.zeros((width, width), BF16)
    for c in range(clusters):
        ob[c] = jnp.transpose(
            jnp.broadcast_to(onsite_ref[c : c + 1, :], (width, width))
        )
    sums[...] = jnp.zeros_like(sums)

    def copies(phase):
        return {
            o: pltpu.make_async_remote_copy(
                src_ref=pack.at[phase, o],
                dst_ref=gath.at[phase, pl.ds(4 * o, 4)],
                send_sem=send_sem.at[phase, o],
                recv_sem=recv_sem.at[phase, o],
                device_id=targets[o],
                device_id_type=MESH,
            )
            for o in OTHERS
        }

    sends = [copies(phase) for phase in range(2 * fields)]

    def fill(phase, o, read):
        def one(s, _):
            block = read(readers_ref[0, o, s])
            if o == 3:
                gath[phase, 12 + s] = block
            else:
                pack[phase, o, s] = block
            return 0

        lax.fori_loop(0, 4, one, 0)

    def from_right(f):
        return lambda c: r0[f][c].astype(BF16)

    def from_w(f):
        return lambda c: wb[f, c]

    def send(phase):
        for o in OTHERS:
            sends[phase][o].start()

    for f in range(fields):
        loads[f].wait()
        for o in OTHERS:
            fill(f, o, from_right(f))
        if f == 0:
            pl.semaphore_wait(barrier, len(everyone))
        send(f)
    for f in range(fields):
        fill(f, 3, from_right(f))

    loads[3].wait()
    loads[4].wait()
    inv_copy.wait()

    def lay(c, _):
        for s in range(slots):
            kc[pl.ds(c * 256, width), s * width : (s + 1) * width] = ks[inv_s[c, s]]
            kc[pl.ds(c * 256 + width, width), s * width : (s + 1) * width] = corr[inv_s[8 + c, s]]
        return 0

    lax.fori_loop(0, clusters, lay, 0)
    energies = energies_ref[0:1, :]

    def fold(block):
        return jnp.sum(block.reshape(width // 8, 8, width), axis=0)

    def product(phase, then):
        block = gath[phase].reshape(slots * width, width)

        def part(i, _):
            out = jnp.dot(kc[pl.ds(pl.multiple_of(i * 1024, 1024), 1024), :], block, preferred_element_type=F32)
            for j in range(4):
                then(4 * i + j, out[j * 256 : j * 256 + 128] - energies * out[j * 256 + 128 : j * 256 + 256])
            return 0

        lax.fori_loop(0, 2, part, 0)

    def reduce_start(mine, got, which, stage):
        found = []
        group = groups[stage]
        for distance, device in enumerate(group, 1):
            copy = pltpu.make_async_remote_copy(
                src_ref=mine,
                dst_ref=got.at[len(group) - distance],
                send_sem=psend.at[which, stage, distance],
                recv_sem=precv.at[which, stage, len(group) - distance],
                device_id=device,
                device_id_type=MESH,
            )
            copy.start()
            found.append(copy)
        return found

    for f in range(fields):
        for o in OTHERS:
            sends[f][o].wait_recv()

        def first_then(c, coupled):
            r = r0[f][c]
            image = ob[c] * r + coupled
            y[f, c] = image
            wb[f, c] = (r - STEP * image).astype(BF16)
            sums[f] += fold(r * r)
            sums[3 + f] += fold(r * image)
            sums[6 + f] += fold(image * image)

        product(f, first_then)
        for o in OTHERS + (3,):
            fill(fields + f, o, from_w(f))
        if f < fields - 1:
            send(fields + f)
    for i in range(9):
        part1[i : i + 1, :] = jnp.sum(sums[i], axis=0, keepdims=True)
    part1[9:16, :] = jnp.zeros((7, 128), F32)
    stage_a = reduce_start(part1, got1a, 0, 0)
    for copy in stage_a:
        copy.wait_recv()
    part1b[...] = part1[...] + jnp.sum(got1a[...], axis=0)
    stage_b = reduce_start(part1b, got1b, 0, 1)
    send(2 * fields - 1)

    def second_then_of(f):
        def second_then(c, coupled):
            im[f, c] = ob[c] * (r0[f][c] - STEP * y[f, c]) + coupled

        return second_then

    for o in OTHERS:
        sends[fields][o].wait_recv()
    product(fields, second_then_of(0))

    for copy in stage_b:
        copy.wait_recv()
    whole = jnp.sum(part1b[...] + jnp.sum(got1b[...], axis=0), axis=1, keepdims=True)
    alpha, beta, gain, rr1 = [], [], [], []
    for f in range(fields):
        rr0, b0, yy = whole[f : f + 1], whole[3 + f : 4 + f], whole[6 + f : 7 + f]
        a = rr0 / b0
        n = rr0 + a * (a * yy - 2.0 * b0)
        alpha.append(a)
        rr1.append(n)
        beta.append(n / rr0)
        gain.append(a / STEP)

    for f in range(fields):
        if f > 0:
            for o in OTHERS:
                sends[fields + f][o].wait_recv()
            product(fields + f, second_then_of(f))
        keep = 1.0 - gain[f] + beta[f]

        def combine(c, total):
            r, image = r0[f][c], y[f, c]
            later = r - alpha[f] * image
            direction = later + beta[f] * r
            image = gain[f] * im[f, c] + keep * image
            y[f, c] = later
            dd[f, c] = direction
            im[f, c] = image
            return total + fold(direction * image)

        total = lax.fori_loop(0, clusters, combine, jnp.zeros((8, 128), F32))
        part2[f : f + 1, :] = jnp.sum(total, axis=0, keepdims=True)
    part2[3:8, :] = jnp.zeros((5, 128), F32)

    last_a = reduce_start(part2, got2a, 1, 0)
    for copy in last_a:
        copy.wait_recv()
    part2b[...] = part2[...] + jnp.sum(got2a[...], axis=0)
    last_b = reduce_start(part2b, got2b, 1, 1)
    for copy in last_b:
        copy.wait_recv()
    whole = jnp.sum(part2b[...] + jnp.sum(got2b[...], axis=0), axis=1, keepdims=True)

    outs = []
    for f in range(fields):
        step = rr1[f] / whole[f : f + 1]

        def finish(c, _):
            dd[f, c] = alpha[f] * r0[f][c] + step * dd[f, c]
            y[f, c] = y[f, c] - step * im[f, c]
            return 0

        lax.fori_loop(0, clusters, finish, 0)
        outs.append(pltpu.make_async_copy(dd.at[f], x_hbm.at[f], out_sem.at[f]))
        outs.append(pltpu.make_async_copy(y.at[f], res_hbm.at[f], out_sem.at[3 + f]))
        outs[-2].start()
        outs[-1].start()
    for phase in sends:
        for copy in phase.values():
            copy.wait_send()
    for copy in stage_a + stage_b + last_a + last_b:
        copy.wait_send()
    for copy in outs:
        copy.wait()


def body(right_side, onsite, energies, ks_tiles, correlation_tiles, tile_slot, readers):
    fields = right_side.shape[0]
    any_, vmem, smem = pl.ANY, pltpu.VMEM, pltpu.SMEM
    spaces = (any_, vmem, vmem, any_, any_, vmem, smem)
    field = (fields, 8, 128, 128)
    scratch = [
        pltpu.VMEM(field[1:], F32),
        pltpu.VMEM(field[1:], F32),
        pltpu.VMEM(field[1:], F32),
        pltpu.VMEM(field, F32),
        pltpu.VMEM(field, F32),
        pltpu.VMEM(field, F32),
        pltpu.VMEM(field[1:], F32),
        pltpu.VMEM(field, BF16),
        pltpu.VMEM((2048, 3584), BF16),
        pltpu.VMEM((193, 128, 128), BF16),
        pltpu.VMEM((65, 128, 128), BF16),
        pltpu.VMEM((6, 28, 128, 128), BF16),
        pltpu.VMEM((6, 7, 4, 128, 128), BF16),
        pltpu.VMEM((16, 128), jnp.int32),
        pltpu.SMEM((16, 128), jnp.int32),
        pltpu.VMEM((9, 8, 128), F32),
        pltpu.VMEM((16, 128), F32),
        pltpu.VMEM((15, 16, 128), F32),
        pltpu.VMEM((16, 128), F32),
        pltpu.VMEM((15, 16, 128), F32),
        pltpu.VMEM((8, 128), F32),
        pltpu.VMEM((15, 8, 128), F32),
        pltpu.VMEM((8, 128), F32),
        pltpu.VMEM((15, 8, 128), F32),
        pltpu.SemaphoreType.DMA((5,)),
        pltpu.SemaphoreType.DMA,
        pltpu.SemaphoreType.DMA((6,)),
        pltpu.SemaphoreType.DMA((6, 7)),
        pltpu.SemaphoreType.DMA((6, 7)),
        pltpu.SemaphoreType.DMA((2, 2, 16)),
        pltpu.SemaphoreType.DMA((2, 2, 16)),
    ]
    x, res = pl.pallas_call(
        kernel,
        out_shape=(jax.ShapeDtypeStruct(field, F32),) * 2,
        in_specs=[pl.BlockSpec(memory_space=s) for s in spaces],
        out_specs=(pl.BlockSpec(memory_space=any_),) * 2,
        scratch_shapes=scratch,
        compiler_params=pltpu.CompilerParams(
            collective_id=0, has_side_effects=True, vmem_limit_bytes=56 << 20
        ),
    )(
        right_side.reshape(field),
        onsite.reshape(8, 128),
        energies.reshape(1, 128),
        ks_tiles.reshape(192, 128, 128),
        correlation_tiles.reshape(64, 128, 128),
        tile_slot,
        readers,
    )
    return x.reshape(right_side.shape), res.reshape(right_side.shape)


def solution(mesh):
    placed = (
        P(None, "row", "col"),
        P("row"),
        P("col"),
        P("row", None, None, None),
        P("row", None, None, None),
        P("row", None),
        P("row", None, None),
    )
    return jax.shard_map(
        body,
        mesh=mesh,
        in_specs=placed,
        out_specs=(P(None, "row", "col"), P(None, "row", "col")),
        check_vma=False,
    )
```

time: 482 us -> 93 us (0.19)
  blocking collectives: 228 us -> 0 us
  local copies, waits for them, and re-layouts: 92.7 us -> 5.27 us
  Pallas kernels: 0 us -> 86.9 us
  waiting for transfers between devices: 82.5 us -> 0 us
  matrix products: 39.8 us -> 0 us
  starting transfers between devices: 20.5 us -> 0 us
  other arithmetic: 15.7 us -> 0 us
    psum x3 -> x0, blocking collectives: 228 us -> none  [the longest x2 150 us: squares(): return lax.psum(jnp.sum(vector * vector, axis=(1, 2)), ('row', 'col'))]
    pallas_call x0 -> x1, Pallas kernels: none -> 86.9 us  [body(): pl.pallas_call(kernel, out_shape=(jax.ShapeDtypeStruct(field, F32),) * 2,...]
    ppermute x12 -> x0, waiting for transfers between devices: 82.5 us -> none  [shifted(): lax.ppermute(array, axis, [(i, (i + by) % count) for i in range(count)])]
    dot_general x5 -> x0, matrix products: 39.8 us -> none  [the longest x2 18.2 us: body(): jnp.einsum('rk,fkj->frj', dense_ks, gathered, preferred_element_type=jnp....]
    reshape x6 -> x0, local copies, waits for them, and re-layouts: 30.6 us -> none  [the longest x1 12.8 us: body(): dense_ks.astype(jnp.bfloat16).reshape(clusters * width, slots * width)]
    ppermute x12 -> x0, starting transfers between devices: 20.5 us -> none  [shifted(): lax.ppermute(array, axis, [(i, (i + by) % count) for i in range(count)])]
    another operation x6 -> x0, local copies, waits for them, and re-layouts: 18.6 us -> none  [body(): received = jnp.stack(pieces, 1)]
    gather x4 -> x0, local copies, waits for them, and re-layouts: 16.4 us -> none  [the longest x2 11.4 us: body(): gathered.reshape(fields, slots, width, orbitals)[:, correlation_slot]]
  transfers between devices with their start and end apart: 12 -> 0, of which waited for: 8 -> 0; matrix products, arithmetic and copies ran while one was open for 7% -> 0% of each run, Pallas kernels for 0% -> 0%
where the time goes in v1:
time: 93 us; the launch traced here: 92.8 us
  Pallas kernels  86.9 us (93%)
  local copies, waits for them, and re-layouts  5.27 us (6%)
    pallas_call x1, Pallas kernels, body(): pl.pallas_call(kernel, out_shape=(jax.ShapeDtypeStruct(field, F32),) * 2,...  86.9 us
    unnamed x5, local copies, waits for them, and re-layouts  5.27 us

profile of v1, /device:TPU:1, one launch (start us, length us, event | category | flops | bytes accessed | tf_op | source)
XLA Modules:
  0.0 92.8 jit_solution(17566208529317261715)
XLA Ops:
  0.6 1.4 %copy.9.readers_ref = s32[1,7,4]{2,1,0:T(8,128)} copy(s32[1,7,4]{1,2,0:T(4,128)} %param.13) | data formatting | bytes 224 | tf_op args[6]
  2.0 86.9 %shard_map.86 = (f32[3,8,128,128]{3,2,1,0:T(8,128)}, f32[3,8,128,128]{3,2,1,0:T(8,128)}) custom-call(f32[3,8,128,128]{3,2,1,0:T(8,128)} %bitcast.11, f32[8,128]{1,0:T(8,128)} %bitcast.12, f32[1,128]{1,0:T(1,128)} %bitcast.13, bf16[192,128,128]{2,1,0:T(8,128)(2,1)} %bitcast.7, bf16[64,128,128]{2,1,0:T(8,128)(2,1)} %bitcast.8, s32[8,24]{1,0:T(8,128)} %slot_ref.1, ...), custom_call_target="tpu_custom_call" | custom-call | tf_op jit(solution)/shard_map/pallas_call | solution.py:316
  88.9 0.0 copy-start
  88.9 2.8 %copy.12 = f32[3,1024,128]{2,1,0:T(8,128)} copy(f32[3,1024,128]{2,1,0:T(8,128)} %bitcast.10) | data formatting | bytes 3145728
  91.7 0.0 copy-done
  91.7 1.1 %copy.13 = f32[3,1024,128]{2,1,0:T(8,128)} copy(f32[3,1024,128]{2,1,0:T(8,128)S(1)} %bitcast.9) | data formatting | bytes 3145728
Async XLA Ops:
  88.9 2.8 %copy-start = (f32[3,8,128,128]{3,2,1,0:T(8,128)S(1)}, f32[3,8,128,128]{3,2,1,0:T(8,128)}, u32[]{:S(2)}) copy-start(f32[3,8,128,128]{3,2,1,0:T(8,128)} %get-tuple-element.5) | copy-start | bytes 4718596

commit v2 on v0

v2 whole, which is shorter than its diff:
```python
import jax
import jax.numpy as jnp
from jax import lax
from jax.experimental import pallas as pl
from jax.experimental.pallas import tpu as pltpu
from jax.sharding import PartitionSpec as P

MESH = pl.DeviceIdType.MESH
F32 = jnp.float32
BF16 = jnp.bfloat16
SIZES = {"x": 4, "y": 4, "z": 8, "core": 2}
GROUPS = (("x", "y"), ("z", "core"))
STEP = 1.0 / 12.0
OWN, SIB, OUT2, IN2, IN3, OUT1, OUT3 = range(7)
FULL = 7


def members(axes, here):
    count, mine = 1, 0
    for a in axes:
        count *= SIZES[a]
        mine = mine * SIZES[a] + here[a]
    found = []
    for distance in range(1, count):
        there, rest = dict(here), lax.rem(mine + distance, count)
        for a in reversed(axes):
            there[a] = lax.rem(rest, SIZES[a])
            rest = rest // SIZES[a]
        found.append(((there["y"] * SIZES["z"] + there["z"]) * SIZES["core"] + there["core"], there["x"]))
    return found


def kernel(
    right_hbm, onsite_ref, energies_ref, ks_hbm, corr_hbm, slot_ref, readers_ref,
    y, z, coef_ref,
    r0a, r0b, r0c, ob, vb, kc, ks, corr, acc, gath, pack,
    full0, full1, full2, full3, full4,
    inv_v, inv_s, mine_v, mine_s, theirs_v, theirs_s, sums,
    part, got, partb, gotb,
    load_sem, table_sem, send_sem, recv_sem, psend, precv,
):
    r0 = (r0a, r0b, r0c)
    full = (full0, full1, full2, full3, full4)
    fields = len(r0)
    last = 2 * fields - 1
    clusters, width, slots = 8, 128, 28
    n_row = lax.axis_size("row")
    row, col = lax.axis_index("row"), lax.axis_index("col")
    core = lax.rem(row, 2)
    s = 2 * core - 1
    here = {"x": col, "y": row // 16, "z": lax.rem(row // 2, 8), "core": core}
    groups = [members(g, here) for g in GROUPS]

    def away(d):
        return (lax.rem(row + d + n_row, n_row), col)

    barrier = pltpu.get_barrier_semaphore()
    everyone = [away(d * s) for d in (-3, -2, -1, 1, 2, 3)] + groups[0] + groups[1]
    for device in everyone:
        pl.semaphore_signal(barrier, 1, device_id=device, device_id_type=MESH)

    loads = [pltpu.make_async_copy(right_hbm.at[f], r0[f], load_sem.at[f]) for f in range(fields)]
    loads.append(pltpu.make_async_copy(ks_hbm, ks.at[pl.ds(0, 192)], load_sem.at[3]))
    loads.append(pltpu.make_async_copy(corr_hbm, corr.at[pl.ds(0, 64)], load_sem.at[4]))
    for load in loads:
        load.start()

    mine_v[...] = jnp.zeros_like(mine_v)
    mine_v[0:4, 0:7] = readers_ref[...]
    mine_copy = pltpu.make_async_copy(mine_v, mine_s, table_sem.at[0])
    mine_copy.start()

    lane = lax.broadcasted_iota(jnp.int32, (8, 128), 1)
    first = lax.broadcasted_iota(jnp.int32, (8, 128), 0)
    at_ks = jnp.full((8, 128), 192, jnp.int32)
    at_corr = jnp.full((8, 128), 64, jnp.int32)
    for k in range(24):
        hit = lane == slot_ref[:, k : k + 1]
        at_ks = jnp.where(hit, first * 24 + k, at_ks)
        if k < 8:
            at_corr = jnp.where(hit, first * 8 + k, at_corr)
    inv_v[0:8] = at_ks
    inv_v[8:16] = at_corr
    inv_copy = pltpu.make_async_copy(inv_v, inv_s, table_sem.at[1])
    inv_copy.start()
    ks[192] = jnp.zeros((width, width), BF16)
    corr[64] = jnp.zeros((width, width), BF16)
    sums[...] = jnp.zeros_like(sums)

    def remote(phase, kind, src, dst, d):
        return pltpu.make_async_remote_copy(
            src_ref=src,
            dst_ref=dst,
            send_sem=send_sem.at[phase, kind],
            recv_sem=recv_sem.at[phase, kind],
            device_id=away(d * s),
            device_id_type=MESH,
        )

    straight = {SIB: -1, IN2: -2, IN3: -3, OUT1: 1, OUT2: 2, OUT3: 3}
    copies = []
    for phase in range(2 * fields):
        passed = phase < last
        found = {}
        for kind, d in straight.items():
            if passed and kind == OUT2:
                continue
            hop = d - 2 if passed and kind in (OUT1, OUT3) else d
            found[kind] = remote(phase, kind, pack.at[phase, kind], gath.at[phase, pl.ds(4 * kind, 4)], hop)
        if passed:
            found[FULL] = remote(phase, FULL, vb.at[phase], full[phase], 2)
        copies.append(found)
    table = pltpu.make_async_remote_copy(
        src_ref=mine_v,
        dst_ref=theirs_v,
        send_sem=table_sem.at[2],
        recv_sem=table_sem.at[3],
        device_id=away(2 * s),
        device_id_type=MESH,
    )

    def fill(phase, kind, read, names, o):
        def one(i, _):
            block = read(names[i, o])
            if kind in (OWN, FULL):
                gath[phase, (4 * OWN if kind == OWN else 4 * OUT2) + i] = block
            else:
                pack[phase, kind, i] = block
            return 0

        lax.fori_loop(0, 4, one, 0)

    def fill_mine(phase, kinds):
        for kind in kinds:
            o = 3 if kind == OWN else 3 - straight[kind] * s
            fill(phase, kind, lambda c: vb[phase, c], mine_s, o)

    def start(phase, kinds):
        for kind in kinds:
            copies[phase][kind].start()

    def wait(phase, kinds):
        for kind in kinds:
            copies[phase][kind].wait_recv()

    def send_out(phase):
        start(phase, (FULL,))
        fill_mine(phase, (SIB, IN3, IN2))
        start(phase, (IN3, IN2, SIB))

    def pass_on(phase):
        wait(phase, (FULL,))
        read = lambda c: full[phase][c]
        fill(phase, OUT3, read, theirs_s, 3 - 3 * s)
        start(phase, (OUT3,))
        fill(phase, OUT1, read, theirs_s, 3 - s)
        start(phase, (OUT1,))
        fill(phase, FULL, read, theirs_s, 3 - 2 * s)

    def halve(f):
        def one(c, _):
            vb[f, c] = r0[f][c].astype(BF16)
            return 0

        lax.fori_loop(0, clusters, one, 0)

    loads[0].wait()
    halve(0)
    mine_copy.wait()
    fill_mine(0, (SIB, IN3, IN2))
    pl.semaphore_wait(barrier, len(everyone))
    table.start()
    start(0, (FULL, IN3, IN2, SIB))
    loads[1].wait()
    halve(1)
    send_out(1)
    loads[2].wait()
    halve(2)
    fill_mine(2, (SIB, IN3, IN2))
    for f in range(fields):
        fill_mine(f, (OWN,))
    for c in range(clusters):
        ob[c] = jnp.transpose(jnp.broadcast_to(onsite_ref[c : c + 1, :], (width, width)))

    loads[3].wait()
    loads[4].wait()
    inv_copy.wait()
    offsets = [3, 3 - s, 3 - 2 * s, 3 + 2 * s, 3 - 3 * s, 3 + s, 3 + 3 * s]

    def lay(c, _):
        for kind in range(7):
            for i in range(4):
                slot = 4 * offsets[kind] + i
                at = slice((4 * kind + i) * width, (4 * kind + i + 1) * width)
                kc[pl.ds(c * 256, width), at] = ks[inv_s[c, slot]]
                kc[pl.ds(c * 256 + width, width), at] = corr[inv_s[8 + c, slot]]
        return 0

    lax.fori_loop(0, clusters, lay, 0)
    table.wait_recv()
    theirs_copy = pltpu.make_async_copy(theirs_v, theirs_s, table_sem.at[4])
    theirs_copy.start()
    theirs_copy.wait()
    energies = energies_ref[0:1, :]

    def fold(block):
        return jnp.sum(block.reshape(width // 8, 8, width), axis=0)

    def product(phase, a, b, where, fresh, then=None):
        block = gath[phase, 4 * a : 4 * b].reshape(4 * (b - a) * width, width)

        def part(i, _):
            at = pl.ds(pl.multiple_of(i * 1024, 1024), 1024)
            out = jnp.dot(kc[at, 4 * a * width : 4 * b * width], block, preferred_element_type=F32)
            if not fresh:
                out = out + acc[where, at, :]
            if then is None:
                acc[where, at, :] = out
            else:
                for j in range(4):
                    then(4 * i + j, out[j * 256 : j * 256 + 128] - energies * out[j * 256 + 128 : j * 256 + 256])
            return 0

        lax.fori_loop(0, 2, part, 0)

    def reduce_start(mine, got, stage):
        group = groups[stage]
        for distance, device in enumerate(group, 1):
            pltpu.make_async_remote_copy(
                src_ref=mine,
                dst_ref=got.at[len(group) - distance],
                send_sem=psend.at[stage],
                recv_sem=precv.at[stage],
                device_id=device,
                device_id_type=MESH,
            ).start()
        return pltpu.make_async_remote_copy(
            src_ref=got,
            dst_ref=got,
            send_sem=psend.at[stage],
            recv_sem=precv.at[stage],
            device_id=group[0],
            device_id_type=MESH,
        )

    def first_then_of(f):
        def first_then(c, coupled):
            r = r0[f][c]
            image = ob[c] * r + coupled
            y[f, c] = image
            vb[fields + f, c] = (r - STEP * image).astype(BF16)
            sums[f] += fold(r * r)
            sums[3 + f] += fold(r * image)
            sums[6 + f] += fold(image * image)

        return first_then

    def second_then_of(f):
        def second_then(c, coupled):
            r = r0[f][c]
            w = r - STEP * y[f, c]
            image = ob[c] * w + coupled
            z[f, c] = image
            sums[9 + f] += fold(w * image)
            sums[12 + f] += fold(r * image)

        return second_then

    def early(phase, where):
        wait(phase, (SIB, IN2, IN3))
        product(phase, OWN, OUT1, where, True)

    def late(phase, where, then):
        wait(phase, (OUT1, OUT3))
        product(phase, OUT1, 7, where, False, then)

    pass_on(0)
    start(2, (FULL, IN3, IN2, SIB))
    early(0, 0)
    pass_on(1)
    late(0, 0, first_then_of(0))
    send_out(3)
    early(1, 1)
    pass_on(2)
    late(1, 1, first_then_of(1))
    send_out(4)
    fill_mine(3, (OWN,))
    early(2, 2)
    pass_on(3)
    late(2, 2, first_then_of(2))
    fill_mine(last, (OUT3, OUT2))
    start(last, (OUT3, OUT2))

    fill_mine(last, (SIB, OUT1, IN2, IN3, OWN))
    start(last, (SIB,))
    early(3, 0)
    pass_on(4)
    start(last, (OUT1, IN2, IN3))
    fill_mine(4, (OWN,))
    early(4, 1)
    late(3, 0, second_then_of(0))
    wait(last, (SIB,))
    product(last, OWN, OUT2, 2, True)
    wait(last, (OUT2,))
    product(last, OUT2, IN2, 2, False)
    wait(last, (OUT3,))
    product(last, OUT3, 7, 2, False)
    late(4, 1, second_then_of(1))
    wait(last, (OUT1,))
    product(last, OUT1, OUT3, 2, False)
    wait(last, (IN2,))
    product(last, IN2, IN3, 2, False)
    wait(last, (IN3,))
    product(last, IN3, OUT1, 2, False, second_then_of(2))

    corner = lax.broadcasted_iota(jnp.int32, (16, 128), 0) == lax.broadcasted_iota(jnp.int32, (16, 128), 1)
    column = jnp.sum(jnp.sum(sums[...], axis=1), axis=1, keepdims=True)
    part[...] = jnp.sum(jnp.where(corner, column, 0.0), axis=0, keepdims=True)
    stage_a = reduce_start(part, got, 0)
    for phase in copies:
        for copy in phase.values():
            copy.wait_send()
    table.wait_send()
    stage_a.wait_recv()
    partb[...] = part[...] + jnp.sum(got[...], axis=0)
    stage_b = reduce_start(partb, gotb, 1)
    stage_a.wait_send()
    stage_b.wait_recv()
    row_sums = partb[...] + jnp.sum(gotb[...], axis=0)
    whole = jnp.sum(jnp.where(corner, row_sums, 0.0), axis=1, keepdims=True)
    rr0, b0, yy, wz, rz = (whole[3 * i : 3 * i + 3] for i in range(5))
    alpha = rr0 / b0
    rr1 = rr0 + alpha * (alpha * yy - 2.0 * b0)
    gain = alpha / STEP
    keep = 1.0 - gain + rr1 / rr0
    bend = gain * gain * wz + gain * keep * (b0 - STEP * yy + rz) + keep * keep * b0
    step = rr1 / bend
    given = (alpha + step * (gain + keep), -step * gain * STEP, -(alpha + step * keep), -step * gain)
    for i, value in enumerate(given):
        coef_ref[3 * i : 3 * i + 3, :] = jnp.broadcast_to(value, (3, 128))
    coef_ref[12:16, :] = jnp.zeros((4, 128), F32)
    stage_b.wait_send()


def finish(right_hbm, y, z, coef_ref, x_hbm, res_hbm, r0, x, res, load_sem, out_sem):
    fields = y.shape[0]
    loads = [pltpu.make_async_copy(right_hbm.at[f], r0.at[f], load_sem.at[f]) for f in range(fields)]
    for load in loads:
        load.start()
    outs = []
    for f in range(fields):
        a, b, c, d = (coef_ref[3 * i + f : 3 * i + f + 1, :] for i in range(4))
        loads[f].wait()
        for half in range(2):

            def one(i, _):
                i = 4 * half + i
                r, image = r0[f, i], y[f, i]
                x[f, i] = a * r + b * image
                res[f, i] = r + c * image + d * z[f, i]
                return 0

            lax.fori_loop(0, 4, one, 0)
            at = pl.ds(4 * half, 4)
            for array, out, which in ((x, x_hbm, 0), (res, res_hbm, 1)):
                outs.append(pltpu.make_async_copy(array.at[f, at], out.at[f, at], out_sem.at[which, f, half]))
                outs[-1].start()
    for out in outs:
        out.wait()


def body(right_side, onsite, energies, ks_tiles, correlation_tiles, tile_slot, readers):
    fields = right_side.shape[0]
    any_, vmem = pl.ANY, pltpu.VMEM
    spaces = (any_, vmem, vmem, any_, any_, vmem, vmem)
    field = (fields, 8, 128, 128)
    scratch = [
        pltpu.VMEM(field[1:], F32),
        pltpu.VMEM(field[1:], F32),
        pltpu.VMEM(field[1:], F32),
        pltpu.VMEM(field[1:], F32),
        pltpu.VMEM((6, 8, 128, 128), BF16),
        pltpu.VMEM((2048, 3584), BF16),
        pltpu.VMEM((193, 128, 128), BF16),
        pltpu.VMEM((65, 128, 128), BF16),
        pltpu.VMEM((3, 2048, 128), F32),
        pltpu.VMEM((6, 28, 128, 128), BF16),
        pltpu.VMEM((6, 7, 4, 128, 128), BF16),
        *[pltpu.VMEM((8, 128, 128), BF16) for _ in range(5)],
        pltpu.VMEM((16, 128), jnp.int32),
        pltpu.SMEM((16, 128), jnp.int32),
        pltpu.VMEM((8, 128), jnp.int32),
        pltpu.SMEM((8, 128), jnp.int32),
        pltpu.VMEM((8, 128), jnp.int32),
        pltpu.SMEM((8, 128), jnp.int32),
        pltpu.VMEM((16, 8, 128), F32),
        pltpu.VMEM((1, 128), F32),
        pltpu.VMEM((15, 1, 128), F32),
        pltpu.VMEM((1, 128), F32),
        pltpu.VMEM((15, 1, 128), F32),
        pltpu.SemaphoreType.DMA((5,)),
        pltpu.SemaphoreType.DMA((5,)),
        pltpu.SemaphoreType.DMA((6, 8)),
        pltpu.SemaphoreType.DMA((6, 8)),
        pltpu.SemaphoreType.DMA((2,)),
        pltpu.SemaphoreType.DMA((2,)),
    ]
    y, z, coef = pl.pallas_call(
        kernel,
        out_shape=(
            pltpu.VMEM(field, F32),
            pltpu.VMEM(field, F32),
            pltpu.VMEM((16, 128), F32),
        ),
        in_specs=[pl.BlockSpec(memory_space=s) for s in spaces],
        out_specs=(pl.BlockSpec(memory_space=vmem),) * 3,
        scratch_shapes=scratch,
        compiler_params=pltpu.CompilerParams(
            collective_id=0, has_side_effects=True, vmem_limit_bytes=59 << 20
        ),
    )(
        right_side.reshape(field),
        onsite.reshape(8, 128),
        energies.reshape(1, 128),
        ks_tiles.reshape(192, 128, 128),
        correlation_tiles.reshape(64, 128, 128),
        tile_slot,
        readers.reshape(7, 4).T,
    )
    x, res = pl.pallas_call(
        finish,
        out_shape=(jax.ShapeDtypeStruct(field, F32),) * 2,
        in_specs=[pl.BlockSpec(memory_space=s) for s in (any_, vmem, vmem, vmem)],
        out_specs=(pl.BlockSpec(memory_space=any_),) * 2,
        scratch_shapes=[pltpu.VMEM(field, F32) for _ in range(3)]
        + [pltpu.SemaphoreType.DMA((3,)), pltpu.SemaphoreType.DMA((2, 3, 2))],
        compiler_params=pltpu.CompilerParams(vmem_limit_bytes=24 << 20),
    )(right_side.reshape(field), y, z, coef)
    return x.reshape(right_side.shape), res.reshape(right_side.shape)


def solution(mesh):
    placed = (
        P(None, "row", "col"),
        P("row"),
        P("col"),
        P("row", None, None, None),
        P("row", None, None, None),
        P("row", None),
        P("row", None, None),
    )
    return jax.shard_map(
        body,
        mesh=mesh,
        in_specs=placed,
        out_specs=(P(None, "row", "col"), P(None, "row", "col")),
        check_vma=False,
    )
```

time: 482 us -> 73.8 us (0.15)
  blocking collectives: 228 us -> 0 us
  local copies, waits for them, and re-layouts: 92.7 us -> 0.01 us
  waiting for transfers between devices: 82.5 us -> 0 us
  Pallas kernels: 0 us -> 73 us
  matrix products: 39.8 us -> 0 us
  starting transfers between devices: 20.5 us -> 0 us
  other arithmetic: 15.7 us -> 0 us
    psum x3 -> x0, blocking collectives: 228 us -> none  [the longest x2 150 us: squares(): return lax.psum(jnp.sum(vector * vector, axis=(1, 2)), ('row', 'col'))]
    ppermute x12 -> x0, waiting for transfers between devices: 82.5 us -> none  [shifted(): lax.ppermute(array, axis, [(i, (i + by) % count) for i in range(count)])]
    pallas_call x0 -> x2, Pallas kernels: none -> 73 us  [the longest x1 71.1 us: body(): pl.pallas_call(kernel, out_shape=(pltpu.VMEM(field, F32), pltpu.VMEM(fiel...]
    dot_general x5 -> x0, matrix products: 39.8 us -> none  [the longest x2 18.2 us: body(): jnp.einsum('rk,fkj->frj', dense_ks, gathered, preferred_element_type=jnp....]
    reshape x6 -> x0, local copies, waits for them, and re-layouts: 30.6 us -> none  [the longest x1 12.8 us: body(): dense_ks.astype(jnp.bfloat16).reshape(clusters * width, slots * width)]
    ppermute x12 -> x0, starting transfers between devices: 20.5 us -> none  [shifted(): lax.ppermute(array, axis, [(i, (i + by) % count) for i in range(count)])]
    another operation x6 -> x0, local copies, waits for them, and re-layouts: 18.6 us -> none  [body(): received = jnp.stack(pieces, 1)]
    unnamed x27 -> x2, local copies, waits for them, and re-layouts: 16.8 us -> 0.01 us
  transfers between devices with their start and end apart: 12 -> 0, of which waited for: 8 -> 0; matrix products, arithmetic and copies ran while one was open for 7% -> 0% of each run, Pallas kernels for 0% -> 0%
where the time goes in v2:
time: 73.8 us; the launch traced here: 73.7 us
  Pallas kernels  73 us (99%)
    pallas_call x1, Pallas kernels, body(): pl.pallas_call(kernel, out_shape=(pltpu.VMEM(field, F32), pltpu.VMEM(fiel...  71.1 us
    pallas_call x1, Pallas kernels, body(): pl.pallas_call(finish, out_shape=(jax.ShapeDtypeStruct(field, F32),) * 2,...  1.96 us

profile of v2, /device:TPU:1, one launch (start us, length us, event | category | flops | bytes accessed | tf_op | source)
XLA Modules:
  0.0 73.7 jit_solution(7135718143372378754)
XLA Ops:
  0.6 0.0 copy-start
  0.6 71.1 %shard_map.86 = (f32[3,8,128,128]{3,2,1,0:T(8,128)S(1)}, f32[3,8,128,128]{3,2,1,0:T(8,128)S(1)}, f32[16,128]{1,0:T(8,128)S(1)}) custom-call(f32[3,8,128,128]{3,2,1,0:T(8,128)} %bitcast.10, f32[8,128]{1,0:T(8,128)} %bitcast.14, f32[1,128]{1,0:T(1,128)} %bitcast.16, bf16[192,128,128]{2,1,0:T(8,128)(2,1)} %bitcast.12, bf16[64,128,128]{2,1,0:T(8,128)(2,1)} %bitcast.13, ...), custom_call_target="tpu_custom_call" | custom-call | tf_op jit(solution)/shard_map/pallas_call | solution.py:408
  71.7 0.0 copy-done
  71.7 2.0 %shard_map.87 = (f32[3,8,128,128]{3,2,1,0:T(8,128)}, f32[3,8,128,128]{3,2,1,0:T(8,128)}) custom-call(f32[3,8,128,128]{3,2,1,0:T(8,128)S(1)} %bitcast.11, f32[3,8,128,128]{3,2,1,0:T(8,128)S(1)} %get-tuple-element.7.y, f32[3,8,128,128]{3,2,1,0:T(8,128)S(1)} %get-tuple-element.8.z, f32[16,128]{1,0:T(8,128)S(1)} %get-tuple-element.9.coef_ref), custom_call_target="tpu_custom_call" | custom-call | tf_op jit(solution)/shard_map/pallas_call | solution.py:430
Async XLA Ops:
  0.6 71.1 %copy-start = (f32[3,1024,128]{2,1,0:T(8,128)S(1)}, f32[3,1024,128]{2,1,0:T(8,128)}, u32[]{:S(2)}) copy-start(f32[3,1024,128]{2,1,0:T(8,128)} %param.7) | copy-start | bytes 4718596

commit v3 on v2

--- a/solution.py
+++ b/solution.py
@@ -32,15 +32,15 @@
 
 def kernel(
     right_hbm, onsite_ref, energies_ref, ks_hbm, corr_hbm, slot_ref, readers_ref,
-    y, z, coef_ref,
-    r0a, r0b, r0c, ob, vb, kc, ks, corr, acc, gath, pack,
-    full0, full1, full2, full3, full4,
+    r0a, r0b, r0c, y, z, coef_ref,
+    ob, vb, kc, ks, corr, acc, gath, pack,
+    full0, full1, full2, full3, full4, full5,
     inv_v, inv_s, mine_v, mine_s, theirs_v, theirs_s, sums,
     part, got, partb, gotb,
     load_sem, table_sem, send_sem, recv_sem, psend, precv,
 ):
     r0 = (r0a, r0b, r0c)
-    full = (full0, full1, full2, full3, full4)
+    full = (full0, full1, full2, full3, full4, full5)
     fields = len(r0)
     last = 2 * fields - 1
     clusters, width, slots = 8, 128, 28
@@ -55,7 +55,7 @@
         return (lax.rem(row + d + n_row, n_row), col)
 
     barrier = pltpu.get_barrier_semaphore()
-    everyone = [away(d * s) for d in (-3, -2, -1, 1, 2, 3)] + groups[0] + groups[1]
+    everyone = [away(d * s) for d in (-3, -2, -1, 1, 2)] + groups[0] + groups[1]
     for device in everyone:
         pl.semaphore_signal(barrier, 1, device_id=device, device_id_type=MESH)
 
@@ -98,17 +98,14 @@
         )
 
     straight = {SIB: -1, IN2: -2, IN3: -3, OUT1: 1, OUT2: 2, OUT3: 3}
+    hops = {SIB: -1, IN2: -2, IN3: -3, OUT1: -1, OUT3: 1}
     copies = []
     for phase in range(2 * fields):
-        passed = phase < last
-        found = {}
-        for kind, d in straight.items():
-            if passed and kind == OUT2:
-                continue
-            hop = d - 2 if passed and kind in (OUT1, OUT3) else d
-            found[kind] = remote(phase, kind, pack.at[phase, kind], gath.at[phase, pl.ds(4 * kind, 4)], hop)
-        if passed:
-            found[FULL] = remote(phase, FULL, vb.at[phase], full[phase], 2)
+        found = {
+            kind: remote(phase, kind, pack.at[phase, kind], gath.at[phase, pl.ds(4 * kind, 4)], d)
+            for kind, d in hops.items()
+        }
+        found[FULL] = remote(phase, FULL, vb.at[phase], full[phase], 2)
         copies.append(found)
     table = pltpu.make_async_remote_copy(
         src_ref=mine_v,
@@ -143,10 +140,7 @@
         for kind in kinds:
             copies[phase][kind].wait_recv()
 
-    def send_out(phase):
-        start(phase, (FULL,))
-        fill_mine(phase, (SIB, IN3, IN2))
-        start(phase, (IN3, IN2, SIB))
+    INWARD = (IN3, IN2, SIB)
 
     def pass_on(phase):
         wait(phase, (FULL,))
@@ -167,16 +161,18 @@
     loads[0].wait()
     halve(0)
     mine_copy.wait()
-    fill_mine(0, (SIB, IN3, IN2))
+    fill_mine(0, INWARD)
     pl.semaphore_wait(barrier, len(everyone))
     table.start()
-    start(0, (FULL, IN3, IN2, SIB))
+    start(0, (FULL,))
     loads[1].wait()
     halve(1)
-    send_out(1)
+    start(1, (FULL,))
     loads[2].wait()
     halve(2)
-    fill_mine(2, (SIB, IN3, IN2))
+    fill_mine(1, INWARD)
+    start(0, INWARD)
+    fill_mine(2, INWARD)
     for f in range(fields):
         fill_mine(f, (OWN,))
     for c in range(clusters):
@@ -197,6 +193,7 @@
         return 0
 
     lax.fori_loop(0, clusters, lay, 0)
+    start(1, INWARD)
     table.wait_recv()
     theirs_copy = pltpu.make_async_copy(theirs_v, theirs_s, table_sem.at[4])
     theirs_copy.start()
@@ -206,19 +203,23 @@
     def fold(block):
         return jnp.sum(block.reshape(width // 8, 8, width), axis=0)
 
-    def product(phase, a, b, where, fresh, then=None):
-        block = gath[phase, 4 * a : 4 * b].reshape(4 * (b - a) * width, width)
+    def product(phases, a, b, wheres, fresh, thens=None):
+        blocks = [gath[phase, 4 * a : 4 * b].reshape(4 * (b - a) * width, width) for phase in phases]
+        block = blocks[0] if len(blocks) == 1 else jnp.concatenate(blocks, axis=1)
 
         def part(i, _):
             at = pl.ds(pl.multiple_of(i * 1024, 1024), 1024)
-            out = jnp.dot(kc[at, 4 * a * width : 4 * b * width], block, preferred_element_type=F32)
-            if not fresh:
-                out = out + acc[where, at, :]
-            if then is None:
-                acc[where, at, :] = out
-            else:
-                for j in range(4):
-                    then(4 * i + j, out[j * 256 : j * 256 + 128] - energies * out[j * 256 + 128 : j * 256 + 256])
+            wide = jnp.dot(kc[at, 4 * a * width : 4 * b * width], block, preferred_element_type=F32)
+            for n, where in enumerate(wheres):
+                out = wide[:, n * width : (n + 1) * width]
+                if not fresh:
+                    out = out + acc[where, at, :]
+                if thens is None:
+                    acc[where, at, :] = out
+                else:
+                    for j in range(4):
+                        coupled = out[j * 256 : j * 256 + 128] - energies * out[j * 256 + 128 : j * 256 + 256]
+                        thens[n](4 * i + j, coupled)
             return 0
 
         lax.fori_loop(0, 2, part, 0)
@@ -266,56 +267,59 @@
 
         return second_then
 
-    def early(phase, where):
-        wait(phase, (SIB, IN2, IN3))
-        product(phase, OWN, OUT1, where, True)
-
-    def late(phase, where, then):
-        wait(phase, (OUT1, OUT3))
-        product(phase, OUT1, 7, where, False, then)
+    def early(phases, wheres):
+        for phase in phases:
+            wait(phase, (SIB, IN2, IN3))
+        product(phases, OWN, OUT1, wheres, True)
+
+    def late(phases, wheres, thens):
+        for phase in phases:
+            wait(phase, (OUT1, OUT3))
+        product(phases, OUT1, 7, wheres, False, thens)
 
     pass_on(0)
-    start(2, (FULL, IN3, IN2, SIB))
-    early(0, 0)
+    start(2, (FULL,))
+    early((0,), (0,))
+    start(2, INWARD)
     pass_on(1)
-    late(0, 0, first_then_of(0))
-    send_out(3)
-    early(1, 1)
+    late((0,), (0,), (first_then_of(0),))
+    start(3, (FULL,))
+    fill_mine(3, INWARD)
+    early((1,), (1,))
+    start(3, INWARD)
     pass_on(2)
-    late(1, 1, first_then_of(1))
-    send_out(4)
-    fill_mine(3, (OWN,))
-    early(2, 2)
+    late((1,), (1,), (first_then_of(1),))
+    start(4, (FULL,))
+    fill_mine(4, INWARD)
+    early((2,), (2,))
+    start(4, INWARD)
+    late((2,), (2,), (first_then_of(2),))
+    start(last, (FULL,))
+    fill_mine(last, INWARD)
+    start(last, INWARD)
     pass_on(3)
-    late(2, 2, first_then_of(2))
-    fill_mine(last, (OUT3, OUT2))
-    start(last, (OUT3, OUT2))
-
-    fill_mine(last, (SIB, OUT1, IN2, IN3, OWN))
-    start(last, (SIB,))
-    early(3, 0)
+    for phase in range(fields, 2 * fields):
+        fill_mine(phase, (OWN,))
+    wait(last, (SIB,))
+    product((last,), OWN, OUT2, (2,), True)
     pass_on(4)
-    start(last, (OUT1, IN2, IN3))
-    fill_mine(4, (OWN,))
-    early(4, 1)
-    late(3, 0, second_then_of(0))
-    wait(last, (SIB,))
-    product(last, OWN, OUT2, 2, True)
-    wait(last, (OUT2,))
-    product(last, OUT2, IN2, 2, False)
-    wait(last, (OUT3,))
-    product(last, OUT3, 7, 2, False)
-    late(4, 1, second_then_of(1))
+    early((3, 4), (0, 1))
+    pass_on(last)
+    wait(last, (IN2, IN3))
+    product((last,), OUT2, OUT1, (2,), False)
+    late((3, 4), (0, 1), (second_then_of(0), second_then_of(1)))
     wait(last, (OUT1,))
-    product(last, OUT1, OUT3, 2, False)
-    wait(last, (IN2,))
-    product(last, IN2, IN3, 2, False)
-    wait(last, (IN3,))
-    product(last, IN3, OUT1, 2, False, second_then_of(2))
-
+    product((last,), OUT1, OUT3, (2,), False)
     corner = lax.broadcasted_iota(jnp.int32, (16, 128), 0) == lax.broadcasted_iota(jnp.int32, (16, 128), 1)
     column = jnp.sum(jnp.sum(sums[...], axis=1), axis=1, keepdims=True)
     part[...] = jnp.sum(jnp.where(corner, column, 0.0), axis=0, keepdims=True)
+    wait(last, (OUT3,))
+    product((last,), OUT3, 7, (2,), False, (second_then_of(2),))
+
+    on_lane = lax.broadcasted_iota(jnp.int32, (1, 128), 1)
+    for i in (11, 14):
+        total = jnp.sum(jnp.sum(sums[i], axis=0, keepdims=True), axis=1, keepdims=True)
+        part[...] = jnp.where(on_lane == i, total, part[...])
     stage_a = reduce_start(part, got, 0)
     for phase in copies:
         for copy in phase.values():
@@ -327,8 +331,8 @@
     stage_a.wait_send()
     stage_b.wait_recv()
     row_sums = partb[...] + jnp.sum(gotb[...], axis=0)
-    whole = jnp.sum(jnp.where(corner, row_sums, 0.0), axis=1, keepdims=True)
-    rr0, b0, yy, wz, rz = (whole[3 * i : 3 * i + 3] for i in range(5))
+    whole = jnp.broadcast_to(row_sums, (8, 128))
+    rr0, b0, yy, wz, rz = (whole if i == 0 else pltpu.roll(whole, 128 - 3 * i, 1) for i in range(5))
     alpha = rr0 / b0
     rr1 = rr0 + alpha * (alpha * yy - 2.0 * b0)
     gain = alpha / STEP
@@ -337,25 +341,20 @@
     step = rr1 / bend
     given = (alpha + step * (gain + keep), -step * gain * STEP, -(alpha + step * keep), -step * gain)
     for i, value in enumerate(given):
-        coef_ref[3 * i : 3 * i + 3, :] = jnp.broadcast_to(value, (3, 128))
-    coef_ref[12:16, :] = jnp.zeros((4, 128), F32)
+        for f in range(fields):
+            coef_ref[3 * i + f : 3 * i + f + 1, :] = jnp.broadcast_to(value[0:1, f : f + 1], (1, 128))
     stage_b.wait_send()
 
 
-def finish(right_hbm, y, z, coef_ref, x_hbm, res_hbm, r0, x, res, load_sem, out_sem):
-    fields = y.shape[0]
-    loads = [pltpu.make_async_copy(right_hbm.at[f], r0.at[f], load_sem.at[f]) for f in range(fields)]
-    for load in loads:
-        load.start()
+def finish(r0a, r0b, r0c, y, z, coef_ref, x_hbm, res_hbm, x, res, out_sem):
     outs = []
-    for f in range(fields):
+    for f, r0 in enumerate((r0a, r0b, r0c)):
         a, b, c, d = (coef_ref[3 * i + f : 3 * i + f + 1, :] for i in range(4))
-        loads[f].wait()
         for half in range(2):
 
             def one(i, _):
                 i = 4 * half + i
-                r, image = r0[f, i], y[f, i]
+                r, image = r0[i], y[f, i]
                 x[f, i] = a * r + b * image
                 res[f, i] = r + c * image + d * z[f, i]
                 return 0
@@ -375,9 +374,6 @@
     spaces = (any_, vmem, vmem, any_, any_, vmem, vmem)
     field = (fields, 8, 128, 128)
     scratch = [
-        pltpu.VMEM(field[1:], F32),
-        pltpu.VMEM(field[1:], F32),
-        pltpu.VMEM(field[1:], F32),
         pltpu.VMEM(field[1:], F32),
         pltpu.VMEM((6, 8, 128, 128), BF16),
         pltpu.VMEM((2048, 3584), BF16),
@@ -386,7 +382,7 @@
         pltpu.VMEM((3, 2048, 128), F32),
         pltpu.VMEM((6, 28, 128, 128), BF16),
         pltpu.VMEM((6, 7, 4, 128, 128), BF16),
-        *[pltpu.VMEM((8, 128, 128), BF16) for _ in range(5)],
+        *[pltpu.VMEM((8, 128, 128), BF16) for _ in range(6)],
         pltpu.VMEM((16, 128), jnp.int32),
         pltpu.SMEM((16, 128), jnp.int32),
         pltpu.VMEM((8, 128), jnp.int32),
@@ -405,15 +401,18 @@
         pltpu.SemaphoreType.DMA((2,)),
         pltpu.SemaphoreType.DMA((2,)),
     ]
-    y, z, coef = pl.pallas_call(
+    r0a, r0b, r0c, y, z, coef = pl.pallas_call(
         kernel,
         out_shape=(
+            pltpu.VMEM(field[1:], F32),
+            pltpu.VMEM(field[1:], F32),
+            pltpu.VMEM(field[1:], F32),
             pltpu.VMEM(field, F32),
             pltpu.VMEM(field, F32),
             pltpu.VMEM((16, 128), F32),
         ),
         in_specs=[pl.BlockSpec(memory_space=s) for s in spaces],
-        out_specs=(pl.BlockSpec(memory_space=vmem),) * 3,
+        out_specs=(pl.BlockSpec(memory_space=vmem),) * 6,
         scratch_shapes=scratch,
         compiler_params=pltpu.CompilerParams(
             collective_id=0, has_side_effects=True, vmem_limit_bytes=59 << 20
@@ -430,12 +429,11 @@
     x, res = pl.pallas_call(
         finish,
         out_shape=(jax.ShapeDtypeStruct(field, F32),) * 2,
-        in_specs=[pl.BlockSpec(memory_space=s) for s in (any_, vmem, vmem, vmem)],
+        in_specs=[pl.BlockSpec(memory_space=s) for s in (vmem,) * 6],
         out_specs=(pl.BlockSpec(memory_space=any_),) * 2,
-        scratch_shapes=[pltpu.VMEM(field, F32) for _ in range(3)]
-        + [pltpu.SemaphoreType.DMA((3,)), pltpu.SemaphoreType.DMA((2, 3, 2))],
+        scratch_shapes=[pltpu.VMEM(field, F32), pltpu.VMEM(field, F32), pltpu.SemaphoreType.DMA((2, 3, 2))],
         compiler_params=pltpu.CompilerParams(vmem_limit_bytes=24 << 20),
-    )(right_side.reshape(field), y, z, coef)
+    )(r0a, r0b, r0c, y, z, coef)
     return x.reshape(right_side.shape), res.reshape(right_side.shape)
 
 

time: 73.8 us -> 71.4 us (0.967)
  Pallas kernels: 73 us -> 70.7 us
    pallas_call x1, Pallas kernels: 71.1 us -> 68.8 us  [body(): pl.pallas_call(kernel, out_shape=(pltpu.VMEM(field[1:], F32), pltpu.VMEM(...]
where the time goes in v3:
time: 71.4 us; the launch traced here: 71.3 us
  Pallas kernels  70.7 us (99%)
    pallas_call x1, Pallas kernels, body(): pl.pallas_call(kernel, out_shape=(pltpu.VMEM(field[1:], F32), pltpu.VMEM(...  68.8 us
    pallas_call x1, Pallas kernels, body(): pl.pallas_call(finish, out_shape=(jax.ShapeDtypeStruct(field, F32),) * 2,...  1.83 us

profile of v3, /device:TPU:1, one launch (start us, length us, event | category | flops | bytes accessed | tf_op | source)
XLA Modules:
  0.0 71.3 jit_solution(9564009695779276894)
XLA Ops:
  0.6 68.8 %shard_map.86 = (f32[8,128,128]{2,1,0:T(8,128)S(1)}, f32[8,128,128]{2,1,0:T(8,128)S(1)}, f32[8,128,128]{2,1,0:T(8,128)S(1)}, f32[3,8,128,128]{3,2,1,0:T(8,128)S(...) custom-call(f32[3,8,128,128]{3,2,1,0:T(8,128)} %bitcast.12, f32[8,128]{1,0:T(8,128)} %bitcast.13, ...), custom_call_target="tpu_custom_call" | custom-call | tf_op jit(solution)/shard_map/pallas_call | solution.py:404
  69.5 1.8 %shard_map.87 = (f32[3,8,128,128]{3,2,1,0:T(8,128)}, f32[3,8,128,128]{3,2,1,0:T(8,128)}) custom-call(f32[8,128,128]{2,1,0:T(8,128)S(1)} %get-tuple-element.10.r0a, f32[8,128,128]{2,1,0:T(8,128)S(1)} %get-tuple-element.11.r0b, f32[8,128,128]{2,1,0:T(8,128)S(1)} %get-tuple-element.12.r0c, f32[3,8,128,128]{3,2,1,0:T(8,128)S(1)} %get-tuple-element.13.y, ...), custom_call_target="tpu_custom_call" | custom-call | tf_op jit(solution)/shard_map/pallas_call | solution.py:429

commit v4 on v3

--- a/solution.py
+++ b/solution.py
@@ -279,20 +279,20 @@
 
     pass_on(0)
     start(2, (FULL,))
+    start(2, INWARD)
     early((0,), (0,))
-    start(2, INWARD)
     pass_on(1)
     late((0,), (0,), (first_then_of(0),))
     start(3, (FULL,))
     fill_mine(3, INWARD)
+    start(3, INWARD)
     early((1,), (1,))
-    start(3, INWARD)
     pass_on(2)
     late((1,), (1,), (first_then_of(1),))
     start(4, (FULL,))
     fill_mine(4, INWARD)
+    start(4, INWARD)
     early((2,), (2,))
-    start(4, INWARD)
     late((2,), (2,), (first_then_of(2),))
     start(last, (FULL,))
     fill_mine(last, INWARD)
@@ -307,9 +307,9 @@
     pass_on(last)
     wait(last, (IN2, IN3))
     product((last,), OUT2, OUT1, (2,), False)
-    late((3, 4), (0, 1), (second_then_of(0), second_then_of(1)))
     wait(last, (OUT1,))
     product((last,), OUT1, OUT3, (2,), False)
+    late((3, 4), (0, 1), (second_then_of(0), second_then_of(1)))
     corner = lax.broadcasted_iota(jnp.int32, (16, 128), 0) == lax.broadcasted_iota(jnp.int32, (16, 128), 1)
     column = jnp.sum(jnp.sum(sums[...], axis=1), axis=1, keepdims=True)
     part[...] = jnp.sum(jnp.where(corner, column, 0.0), axis=0, keepdims=True)

time: 71.4 us -> 70.5 us (0.987)
  Pallas kernels: 70.7 us -> 69.8 us
    pallas_call x1, Pallas kernels: 68.8 us -> 67.9 us  [body(): pl.pallas_call(kernel, out_shape=(pltpu.VMEM(field[1:], F32), pltpu.VMEM(...]
where the time goes in v4:
time: 70.5 us; the launch traced here: 70.4 us
  Pallas kernels  69.8 us (99%)
    pallas_call x1, Pallas kernels, body(): pl.pallas_call(kernel, out_shape=(pltpu.VMEM(field[1:], F32), pltpu.VMEM(...  67.9 us
    pallas_call x1, Pallas kernels, body(): pl.pallas_call(finish, out_shape=(jax.ShapeDtypeStruct(field, F32),) * 2,...  1.83 us

profile of v4, /device:TPU:1, one launch (start us, length us, event | category | flops | bytes accessed | tf_op | source)
XLA Modules:
  0.0 70.4 jit_solution(227921682754955944)
XLA Ops:
  0.6 67.9 %shard_map.86 = (f32[8,128,128]{2,1,0:T(8,128)S(1)}, f32[8,128,128]{2,1,0:T(8,128)S(1)}, f32[8,128,128]{2,1,0:T(8,128)S(1)}, f32[3,8,128,128]{3,2,1,0:T(8,128)S(...) custom-call(f32[3,8,128,128]{3,2,1,0:T(8,128)} %bitcast.12, f32[8,128]{1,0:T(8,128)} %bitcast.13, ...), custom_call_target="tpu_custom_call" | custom-call | tf_op jit(solution)/shard_map/pallas_call | solution.py:404
  68.6 1.8 %shard_map.87 = (f32[3,8,128,128]{3,2,1,0:T(8,128)}, f32[3,8,128,128]{3,2,1,0:T(8,128)}) custom-call(f32[8,128,128]{2,1,0:T(8,128)S(1)} %get-tuple-element.10.r0a, f32[8,128,128]{2,1,0:T(8,128)S(1)} %get-tuple-element.11.r0b, f32[8,128,128]{2,1,0:T(8,128)S(1)} %get-tuple-element.12.r0c, f32[3,8,128,128]{3,2,1,0:T(8,128)S(1)} %get-tuple-element.13.y, ...), custom_call_target="tpu_custom_call" | custom-call | tf_op jit(solution)/shard_map/pallas_call | solution.py:429

commit v5 on v4

--- a/solution.py
+++ b/solution.py
@@ -55,7 +55,7 @@
         return (lax.rem(row + d + n_row, n_row), col)
 
     barrier = pltpu.get_barrier_semaphore()
-    everyone = [away(d * s) for d in (-3, -2, -1, 1, 2)] + groups[0] + groups[1]
+    everyone = groups[0] + groups[1] + [away(d * s) for d in (-3, -2, -1, 1, 2)]
     for device in everyone:
         pl.semaphore_signal(barrier, 1, device_id=device, device_id_type=MESH)
 
@@ -226,7 +226,11 @@
 
     def reduce_start(mine, got, stage):
         group = groups[stage]
-        for distance, device in enumerate(group, 1):
+        inner = SIZES[GROUPS[stage][1]]
+        outer = SIZES[GROUPS[stage][0]]
+        far = lambda d: -min(d // inner, outer - d // inner) - min(d % inner, inner - d % inner)
+        for distance in sorted(range(1, len(group) + 1), key=far):
+            device = group[distance - 1]
             pltpu.make_async_remote_copy(
                 src_ref=mine,
                 dst_ref=got.at[len(group) - distance],

time: 70.5 us -> 70.4 us (level)
  no operation moved by 1% of the time
where the time goes in v5:
time: 70.4 us; the launch traced here: 70.3 us
  Pallas kernels  69.7 us (99%)
    pallas_call x1, Pallas kernels, body(): pl.pallas_call(kernel, out_shape=(pltpu.VMEM(field[1:], F32), pltpu.VMEM(...  67.8 us
    pallas_call x1, Pallas kernels, body(): pl.pallas_call(finish, out_shape=(jax.ShapeDtypeStruct(field, F32),) * 2,...  1.83 us

profile of v5, /device:TPU:1, one launch (start us, length us, event | category | flops | bytes accessed | tf_op | source)
XLA Modules:
  0.0 70.3 jit_solution(15881859664147503472)
XLA Ops:
  0.6 67.8 %shard_map.86 = (f32[8,128,128]{2,1,0:T(8,128)S(1)}, f32[8,128,128]{2,1,0:T(8,128)S(1)}, f32[8,128,128]{2,1,0:T(8,128)S(1)}, f32[3,8,128,128]{3,2,1,0:T(8,128)S(...) custom-call(f32[3,8,128,128]{3,2,1,0:T(8,128)} %bitcast.12, f32[8,128]{1,0:T(8,128)} %bitcast.13, ...), custom_call_target="tpu_custom_call" | custom-call | tf_op jit(solution)/shard_map/pallas_call | solution.py:408
  68.5 1.8 %shard_map.87 = (f32[3,8,128,128]{3,2,1,0:T(8,128)}, f32[3,8,128,128]{3,2,1,0:T(8,128)}) custom-call(f32[8,128,128]{2,1,0:T(8,128)S(1)} %get-tuple-element.10.r0a, f32[8,128,128]{2,1,0:T(8,128)S(1)} %get-tuple-element.11.r0b, f32[8,128,128]{2,1,0:T(8,128)S(1)} %get-tuple-element.12.r0c, f32[3,8,128,128]{3,2,1,0:T(8,128)S(1)} %get-tuple-element.13.y, ...), custom_call_target="tpu_custom_call" | custom-call | tf_op jit(solution)/shard_map/pallas_call | solution.py:433
